TPU v7x, 32 devices: a whole 2x2x4 slice. The times are simulated.
32 devices in a mesh: groups: 2 (over y), row: 4 (over z), col: 4 (over x, core).
Axes of the slice: x: 2, y: 2, z: 4, core: 2. Of those that a mesh axis runs over, the one named last changes fastest.
Arguments:
- tokens: bfloat16 [1024, 4096], P(('groups', 'row'), 'col'), parts along dimension 0, may hold values from -90 to 90
- norm_gain: float32 [4096], P('col'), may hold values from 0.5 to 1.5
- gate_weight: bfloat16 [4096, 16384], P('col', 'row'), may hold values from -0.09375 to 0.09375
- up_weight: bfloat16 [4096, 16384], P('col', 'row'), may hold values from -0.09375 to 0.09375
- down_weight: bfloat16 [16384, 4096], P('row', 'col'), may hold values from -0.046875 to 0.046875
Outputs:
- block_out: bfloat16 [1024, 4096], P(('groups', 'row'), 'col'), parts along dimension 0
There are 2 independent parts, one for each index of `groups`. A program takes and returns all parts, laid end to end along the dimension named above; an argument that names none is the same for every part. Nothing has to cross between parts.
All inputs are finite; a program needn't handle non-finite values.
Results may differ from a plain program's by a relative error of at most 0.02.
Values may be sent and summed in bfloat16 or wider, within the bound.
A program may use at most 128 MiB of HBM per device.

v0:
```python
import jax
import jax.numpy as jnp
from jax import lax
from jax.sharding import PartitionSpec as P

epsilon = 1e-05


def normalize(source, total_squares, width_total, norm_gain):
    inverse_rms = lax.rsqrt(total_squares / width_total + epsilon)
    return (source.astype(jnp.float32) * inverse_rms[:, None] * norm_gain[None, :]).astype(
        jnp.bfloat16
    )


def per_device(tokens, norm_gain, gate_weight, up_weight, down_weight):
    width_total = tokens.shape[1] * lax.axis_size("col")
    split_at = gate_weight.shape[1]
    both_weights = jnp.concatenate([gate_weight, up_weight], axis=1)
    local_squares = jnp.sum(jnp.square(tokens.astype(jnp.float32)), axis=1)
    total_squares = lax.psum(local_squares, "col")
    normed = normalize(tokens, total_squares, width_total, norm_gain)
    gathered = lax.all_gather(normed, "row", axis=0, tiled=True)
    block_rows = gathered
    summed = lax.psum_scatter(
        jnp.dot(block_rows, both_weights, preferred_element_type=jnp.float32).astype(jnp.bfloat16),
        "col",
        scatter_dimension=0,
        tiled=True,
    ).astype(jnp.float32)
    hidden_part = (jax.nn.silu(summed[:, :split_at]) * summed[:, split_at:]).astype(jnp.bfloat16)
    hidden = lax.all_gather(hidden_part, "col", axis=0, tiled=True)
    block_rows = hidden
    return lax.psum_scatter(
        jnp.dot(block_rows, down_weight, preferred_element_type=jnp.float32).astype(jnp.bfloat16),
        "row",
        scatter_dimension=0,
        tiled=True,
    )


def solution(mesh):
    placed = (
        P(("groups", "row"), "col"),
        P("col"),
        P("col", "row"),
        P("col", "row"),
        P("row", "col"),
    )
    return jax.shard_map(
        per_device,
        mesh=mesh,
        in_specs=placed,
        out_specs=P(("groups", "row"), "col"),
        check_vma=False,
    )
```

profile of v0, /device:TPU:0, one launch (start us, length us, event | category | flops | bytes accessed | tf_op | source)
XLA Modules:
  0.0 214.6 jit_solution(8213113644927217040)
XLA Ops:
  6.5 0.0 all-gather.3.cloned.1.call-start
  6.5 1.1 fusion.8
  7.6 8.3 %psum.7 = f32[128]{0:T(128)S(1)} all-reduce(f32[128]{0:T(128)S(1)} %fusion.8), channel_id=1, replica_groups=mesh['groups'=2,'row'=4,'col'=4] {'col'}, use_global_device_ids=true, to_apply=%region_1.0 | all-reduce | flops 128 | bytes 1024 | tf_op jit(solution)/shard_map/psum | solution.py:21
  16.0 1.8 fusion.10
  17.8 0.0 all-gather.3.cloned.1.call-update
  17.8 0.0 reduce-scatter.3.cloned.1.call-start
  17.8 28.4 %all-gather.3.cloned.1.call-done = bf16[512,1024]{1,0:T(8,128)(2,1)} async-done(((bf16[128,1024]{1,0:T(8,128)(2,1)}), bf16[512,1024]{1,0:T(8,128)(2,1)}) %all-gather.3.cloned.1.call-update) | async-done | bytes 1048592 | tf_op jit(solution)/shard_map/all_gather | solution.py:23
  46.2 14.8 %fusion.4 = bf16[512,8192]{1,0:T(8,128)(2,1)} fusion(bf16[512,1024]{1,0:T(8,128)(2,1)} %all-gather.3.cloned.1.call-done, bf16[1024,4096]{1,0:T(8,128)(2,1)} %param.8, bf16[1024,4096]{1,0:T(8,128)(2,1)} %param.7), kind=kOutput, calls=%fused_computation.4 | convolution fusion | flops 8627683328 | bytes 26214400 | tf_op jit(solution)/shard_map/dot_general | solution.py:26
  61.0 0.0 reduce-scatter.3.cloned.1.call-update
  61.0 0.0 all-gather.5.cloned.1.call-start
  61.0 71.3 %reduce-scatter.3.cloned.1.call-done = bf16[128,8192]{1,0:T(8,128)(2,1)} async-done(((bf16[512,8192]{1,0:T(8,128)(2,1)}), bf16[128,8192]{1,0:T(8,128)(2,1)}) %reduce-scatter.3.cloned.1.call-update) | async-done | bytes 2097168 | tf_op jit(solution)/shard_map/reduce_scatter | solution.py:25
  132.4 2.0 convert_element_type.22
  134.4 1.5 fusion.7
  135.9 0.0 all-gather.5.cloned.1.call-update
  135.9 0.0 reduce-scatter.5.cloned.1.call-start
  136.0 34.6 %all-gather.5.cloned.1.call-done = bf16[512,4096]{1,0:T(8,128)(2,1)} async-done(((bf16[128,4096]{1,0:T(8,128)(2,1)}), bf16[512,4096]{1,0:T(8,128)(2,1)}) %all-gather.5.cloned.1.call-update) | async-done | bytes 4194320 | tf_op jit(solution)/shard_map/all_gather | solution.py:32
  170.6 10.1 %convolution_convert_fusion = bf16[512,1024]{1,0:T(8,128)(2,1)} fusion(bf16[512,4096]{1,0:T(8,128)(2,1)} %all-gather.5.cloned.1.call-done, bf16[4096,1024]{1,0:T(8,128)(2,1)} %param.9), kind=kOutput, calls=%fused_computation.7 | convolution fusion | flops 4295491584 | bytes 13631488 | tf_op jit(solution)/shard_map/dot_general | solution.py:35
  180.7 0.0 reduce-scatter.5.cloned.1.call-update
  180.7 27.3 %reduce-scatter.5.cloned.1.call-done = bf16[128,1024]{1,0:T(8,128)(2,1)} async-done(((bf16[512,1024]{1,0:T(8,128)(2,1)}), bf16[128,1024]{1,0:T(8,128)(2,1)}) %reduce-scatter.5.cloned.1.call-update) | async-done | bytes 262160 | tf_op jit(solution)/shard_map/reduce_scatter | solution.py:34
  (1 shorter events, 0.0 us)
Async XLA Ops:
  6.5 39.7 %all-gather.3.cloned.1.call-start = ((), (), s32[]{:S(2)}) async-start(), calls=%async_computation.2 | async-start | bytes 1310720 | tf_op jit(solution)/shard_map/all_gather | solution.py:23
  17.8 114.6 %reduce-scatter.3.cloned.1.call-start = ((), (), s32[]{:S(2)}) async-start(), calls=%async_computation.3 | async-start | bytes 10485760 | tf_op jit(solution)/shard_map/reduce_scatter | solution.py:25
  61.0 109.6 %all-gather.5.cloned.1.call-start = ((), (), s32[]{:S(2)}) async-start(), calls=%async_computation.4 | async-start | bytes 5242880 | tf_op jit(solution)/shard_map/all_gather | solution.py:32
  135.9 72.1 %reduce-scatter.5.cloned.1.call-start = ((), (), s32[]{:S(2)}) async-start(), calls=%async_computation.5 | async-start | bytes 1310720 | tf_op jit(solution)/shard_map/reduce_scatter | solution.py:34
Sparse Core Ops, SparseCore 0:
  17.9 28.2 all-gather.2
  61.1 71.2 reduce-scatter.2
  136.1 34.4 all-gather.4
  180.9 27.1 reduce-scatter.4
where the time goes:
time: 215 us
  waiting for transfers between devices  162 us (75%)
  matrix products  24.9 us (12%)
  between operations  13.1 us (6%)
  blocking collectives  8.34 us (4%)
  other arithmetic  6.43 us (3%)
    reduce_scatter x1, waiting for transfers between devices, per_device(): lax.psum_scatter(jnp.dot(block_rows, both_weights, preferred_element_type...  71.3 us
    all_gather x1, waiting for transfers between devices, per_device(): hidden = lax.all_gather(hidden_part, 'col', axis=0, tiled=True)  34.6 us
    all_gather x1, waiting for transfers between devices, per_device(): gathered = lax.all_gather(normed, 'row', axis=0, tiled=True)  28.4 us
    reduce_scatter x1, waiting for transfers between devices, per_device(): lax.psum_scatter(jnp.dot(block_rows, down_weight, preferred_element_type=...  27.3 us
    dot_general x1, matrix products, per_device(): jnp.dot(block_rows, both_weights, preferred_element_type=jnp.float32)  14.8 us
    dot_general x1, matrix products, per_device(): jnp.dot(block_rows, down_weight, preferred_element_type=jnp.float32)  10.1 us
    psum x1, blocking collectives, per_device(): total_squares = lax.psum(local_squares, 'col')  8.34 us
  transfers between devices with their start and end apart: 4, of which 4 were waited for; matrix products, arithmetic and copies ran while one was open for 0% of the time, Pallas kernels for 0%

commit v1 on v0

--- a/solution.py
+++ b/solution.py
@@ -4,6 +4,19 @@
 from jax.sharding import PartitionSpec as P
 
 epsilon = 1e-05
+
+
+def ring_gather(x, axis, dim):
+    ways = lax.axis_size(axis)
+    up = [(d, (d + 1) % ways) for d in range(ways)]
+    down = [(d, (d - 1) % ways) for d in range(ways)]
+    earlier, later = ([x], [x])
+    for _ in range(ways // 2):
+        earlier.append(lax.ppermute(earlier[-1], axis, up))
+    for _ in range((ways - 1) // 2):
+        later.append(lax.ppermute(later[-1], axis, down))
+    line = jnp.concatenate([*earlier[::-1], *later[1:]], axis=dim)
+    return jnp.roll(line, (lax.axis_index(axis) - ways // 2) * x.shape[dim], axis=dim)
 
 
 def normalize(source, total_squares, width_total, norm_gain):
@@ -20,7 +33,7 @@
     local_squares = jnp.sum(jnp.square(tokens.astype(jnp.float32)), axis=1)
     total_squares = lax.psum(local_squares, "col")
     normed = normalize(tokens, total_squares, width_total, norm_gain)
-    gathered = lax.all_gather(normed, "row", axis=0, tiled=True)
+    gathered = ring_gather(normed, "row", 0)
     block_rows = gathered
     summed = lax.psum_scatter(
         jnp.dot(block_rows, both_weights, preferred_element_type=jnp.float32).astype(jnp.bfloat16),

time: 215 us -> 208 us (0.967)
  waiting for transfers between devices: 162 us -> 149 us
  starting transfers between devices: 0.13 us -> 5.54 us
    all_gather x1 -> x0, waiting for transfers between devices: 28.4 us -> none  [per_device(): gathered = lax.all_gather(normed, 'row', axis=0, tiled=True)]
    ppermute x0 -> x3, waiting for transfers between devices: none -> 14 us  [the longest x2 14 us: ring_gather(): earlier.append(lax.ppermute(earlier[-1], axis, up))]
    ppermute x0 -> x3, starting transfers between devices: none -> 5.45 us  [the longest x1 3.82 us: ring_gather(): later.append(lax.ppermute(later[-1], axis, down))]
  transfers between devices with their start and end apart: 4 -> 6, of which waited for: 4 -> 5; matrix products, arithmetic and copies ran while one was open for 0% -> 1% of each run, Pallas kernels for 0% -> 0%
where the time goes in v1:
time: 208 us
  waiting for transfers between devices  149 us (72%)
  matrix products  24.7 us (12%)
  between operations  13.2 us (6%)
  blocking collectives  8.34 us (4%)
  other arithmetic  7.03 us (3%)
  starting transfers between devices  5.54 us (3%)
    reduce_scatter x1, waiting for transfers between devices, per_device(): lax.psum_scatter(jnp.dot(block_rows, both_weights, preferred_element_type...  72.7 us
    all_gather x1, waiting for transfers between devices, per_device(): hidden = lax.all_gather(hidden_part, 'col', axis=0, tiled=True)  34.6 us
    reduce_scatter x1, waiting for transfers between devices, per_device(): lax.psum_scatter(jnp.dot(block_rows, down_weight, preferred_element_type=...  27.3 us
    dot_general x1, matrix products, per_device(): jnp.dot(block_rows, both_weights, preferred_element_type=jnp.float32)  14.6 us
    ppermute x2, waiting for transfers between devices, ring_gather(): earlier.append(lax.ppermute(earlier[-1], axis, up))  14 us
    dot_general x1, matrix products, per_device(): jnp.dot(block_rows, down_weight, preferred_element_type=jnp.float32)  10.1 us
    psum x1, blocking collectives, per_device(): total_squares = lax.psum(local_squares, 'col')  8.34 us
  transfers between devices with their start and end apart: 6, of which 5 were waited for; matrix products, arithmetic and copies ran while one was open for 1% of the time, Pallas kernels for 0%

profile of v1, /device:TPU:0, one launch (start us, length us, event | category | flops | bytes accessed | tf_op | source)
XLA Modules:
  0.0 207.6 jit_solution(2819930543322083823)
XLA Ops:
  6.5 0.0 copy-start
  6.5 0.0 copy-start.1
  6.5 0.0 reduce-scatter.3.cloned.1.call-start
  6.5 1.1 fusion.9
  7.7 8.3 %psum.7 = f32[128]{0:T(128)S(1)} all-reduce(f32[128]{0:T(128)S(1)} %fusion.9), channel_id=1, replica_groups=mesh['groups'=2,'row'=4,'col'=4] {'col'}, use_global_device_ids=true, to_apply=%region_1.0 | all-reduce | flops 128 | bytes 1024 | tf_op jit(solution)/shard_map/psum | solution.py:34
  16.0 1.1 fusion.11
  17.1 1.6 collective-permute-start
  18.8 7.1 %collective-permute-done = bf16[128,1024]{1,0:T(8,128)(2,1)S(1)} collective-permute-done((bf16[128,1024]{1,0:T(8,128)(2,1)S(1)}, bf16[128,1024]{1,0:T(8,128)(2,1)S(1)}, u32[]{:S(2)}, u32[]{:S(2)}) %collective-permute-start) | collective-permute-done | bytes 262176 | tf_op jit(solution)/shard_map/ppermute | solution.py:15
  25.9 0.0 collective-permute-start.1
  25.9 3.8 %collective-permute-start.2 = (bf16[128,1024]{1,0:T(8,128)(2,1)S(1)}, bf16[128,1024]{1,0:T(8,128)(2,1)S(1)}, u32[]{:S(2)}, u32[]{:S(2)}) collective-permute-start(bf16[128,1024]{1,0:T(8,128)(2,1)S(1)} %fusion.11), channel_id=1, source_target_pairs={{0,12},{4,0},{8,4},{12,8},{1,13},{5,1},{9,5},{13,9},{2,14},{6,2},{... | collective-permute-start | bytes 786440 | tf_op jit(solution)/shard_map/ppermute | solution.py:17
  29.7 6.9 %collective-permute-done.1 = bf16[128,1024]{1,0:T(8,128)(2,1)S(1)} collective-permute-done((bf16[128,1024]{1,0:T(8,128)(2,1)S(1)}, bf16[128,1024]{1,0:T(8,128)(2,1)S(1)}, u32[]{:S(2)}, u32[]{:S(2)}) %collective-permute-start.1) | collective-permute-done | bytes 262176 | tf_op jit(solution)/shard_map/ppermute | solution.py:15
  36.6 1.1 constant_dynamic-update-slice_fusion.5
  37.7 0.0 collective-permute-done.2
  37.8 0.0 copy-done
  37.8 0.0 copy-done.1
  37.8 0.1 constant_dynamic-update-slice_fusion.1
  38.0 14.6 %fusion.4 = bf16[512,8192]{1,0:T(8,128)(2,1)} fusion(bf16[1024,4096]{1,0:T(8,128)(2,1)} %param.8, bf16[1024,4096]{1,0:T(8,128)(2,1)} %param.7, bf16[1024,1024]{1,0:T(8,128)(2,1)S(1)} %constant_dynamic-update-slice_fusion, s32[]{:T(128)S(6)} %select_n.14), kind=kOutput, calls=%fused_computation.4 | convolution fusion | flops 8627683328 | bytes 26214404 | tf_op jit(solution)/shard_map/dot_general | solution.py:39
  52.6 0.0 reduce-scatter.3.cloned.1.call-update
  52.6 0.0 all-gather.2.cloned.1.call-start
  52.7 72.7 %reduce-scatter.3.cloned.1.call-done = bf16[128,8192]{1,0:T(8,128)(2,1)} async-done(((bf16[512,8192]{1,0:T(8,128)(2,1)}), bf16[128,8192]{1,0:T(8,128)(2,1)}) %reduce-scatter.3.cloned.1.call-update) | async-done | bytes 2097168 | tf_op jit(solution)/shard_map/reduce_scatter | solution.py:38
  125.4 2.0 convert_element_type.22
  127.4 1.6 fusion.7
  128.9 0.0 all-gather.2.cloned.1.call-update
  129.0 0.0 reduce-scatter.5.cloned.1.call-start
  129.0 34.6 %all-gather.2.cloned.1.call-done = bf16[512,4096]{1,0:T(8,128)(2,1)} async-done(((bf16[128,4096]{1,0:T(8,128)(2,1)}), bf16[512,4096]{1,0:T(8,128)(2,1)}) %all-gather.2.cloned.1.call-update) | async-done | bytes 4194320 | tf_op jit(solution)/shard_map/all_gather | solution.py:45
  163.6 10.1 %convolution_convert_fusion = bf16[512,1024]{1,0:T(8,128)(2,1)} fusion(bf16[512,4096]{1,0:T(8,128)(2,1)} %all-gather.2.cloned.1.call-done, bf16[4096,1024]{1,0:T(8,128)(2,1)} %param.9), kind=kOutput, calls=%fused_computation.7 | convolution fusion | flops 4295491584 | bytes 13631488 | tf_op jit(solution)/shard_map/dot_general | solution.py:48
  173.7 0.0 reduce-scatter.5.cloned.1.call-update
  173.8 27.3 %reduce-scatter.5.cloned.1.call-done = bf16[128,1024]{1,0:T(8,128)(2,1)} async-done(((bf16[512,1024]{1,0:T(8,128)(2,1)}), bf16[128,1024]{1,0:T(8,128)(2,1)}) %reduce-scatter.5.cloned.1.call-update) | async-done | bytes 262160 | tf_op jit(solution)/shard_map/reduce_scatter | solution.py:47
  (7 shorter events, 0.1 us)
Async XLA Ops:
  6.5 31.3 %copy-start = (bf16[128,1024]{1,0:T(8,128)(2,1)S(1)}, bf16[128,1024]{1,0:T(8,128)(2,1)}, u32[]{:S(2)}) copy-start(bf16[128,1024]{1,0:T(8,128)(2,1)} %param.5) | copy-start | bytes 786436
  6.5 31.3 %copy-start.1 = (f32[1024]{0:T(1024)S(1)}, f32[1024]{0:T(1024)}, u32[]{:S(2)}) copy-start(f32[1024]{0:T(1024)} %param.6) | copy-start | bytes 12292
  6.5 118.8 %reduce-scatter.3.cloned.1.call-start = ((), (), s32[]{:S(2)}) async-start(), calls=%async_computation.2 | async-start | bytes 10485760 | tf_op jit(solution)/shard_map/reduce_scatter | solution.py:38
  17.1 8.8 %collective-permute-start = (bf16[128,1024]{1,0:T(8,128)(2,1)S(1)}, bf16[128,1024]{1,0:T(8,128)(2,1)S(1)}, u32[]{:S(2)}, u32[]{:S(2)}) collective-permute-start(bf16[128,1024]{1,0:T(8,128)(2,1)S(1)} %fusion.11), channel_id=1, source_target_pairs={{0,4},{4,8},{8,12},{12,0},{1,5},{5,9},{9,13},{13,1},{2,6},{6,10},{... | collective-permute-start | bytes 786440 | tf_op jit(solution)/shard_map/ppermute | solution.py:15
  25.9 10.7 %collective-permute-start.1 = (bf16[128,1024]{1,0:T(8,128)(2,1)S(1)}, bf16[128,1024]{1,0:T(8,128)(2,1)S(1)}, u32[]{:S(2)}, u32[]{:S(2)}) collective-permute-start(bf16[128,1024]{1,0:T(8,128)(2,1)S(1)} %collective-permute-done), channel_id=1, source_target_pairs={{0,4},{4,8},{8,12},{12,0},{1,5},{5,9},{9,13},{13,1},{2,6},{6,10},{... | collective-permute-start | bytes 786440 | tf_op jit(solution)/shard_map/ppermute | solution.py:15
  25.9 11.8 %collective-permute-start.2 = (bf16[128,1024]{1,0:T(8,128)(2,1)S(1)}, bf16[128,1024]{1,0:T(8,128)(2,1)S(1)}, u32[]{:S(2)}, u32[]{:S(2)}) collective-permute-start(bf16[128,1024]{1,0:T(8,128)(2,1)S(1)} %fusion.11), channel_id=1, source_target_pairs={{0,12},{4,0},{8,4},{12,8},{1,13},{5,1},{9,5},{13,9},{2,14},{6,2},{... | collective-permute-start | bytes 786440 | tf_op jit(solution)/shard_map/ppermute | solution.py:17
  52.6 111.0 %all-gather.2.cloned.1.call-start = ((), (), s32[]{:S(2)}) async-start(), calls=%async_computation.3 | async-start | bytes 5242880 | tf_op jit(solution)/shard_map/all_gather | solution.py:45
  129.0 72.1 %reduce-scatter.5.cloned.1.call-start = ((), (), s32[]{:S(2)}) async-start(), calls=%async_computation.4 | async-start | bytes 1310720 | tf_op jit(solution)/shard_map/reduce_scatter | solution.py:47
Sparse Core Ops, SparseCore 0:
  52.7 72.6 reduce-scatter.2
  129.1 34.4 all-gather.1
  173.9 27.1 reduce-scatter.4
